TPU v7x, 128 devices: a whole 4x4x4 slice. The times are simulated.
128 devices in a mesh: grp: 4 (over z), aux: 32 (over y, x, core).
Axes of the slice: x: 4, y: 4, z: 4, core: 2. Of those that a mesh axis runs over, the one named last changes fastest.
Arguments:
- three_index: bfloat16 [64, 768, 16384], P(None, None, ('grp', 'aux')), may hold values from -0.25 to 0.25
- block_owner: int32 [64], replicated, may hold values from 0 to 31, as said below
- pair_screen: int32 [64, 64], replicated, may hold values from 0 to 1, as said below
- orbital_counts: int32 [64], replicated, may hold values from 1 to 16, as said below
- occupied_energy: float32 [64, 16], replicated, may hold values from -1.5 to -0.3
- virtual_energy: float32 [64, 48], replicated, may hold values from 0.3 to 2.5
Outputs:
- virtual_density: float32 [64, 48, 48], P('aux', 'grp')
Inputs may be any that keep to these rules, and one draw needn't show every extreme that they name: `block_owner`: every owner index holds 1 to 3 blocks, and some hold exactly 3. `pair_screen`: symmetric, with ones on the diagonal. `orbital_counts`: some block uses all 16 slots.
All inputs are finite; a program needn't handle non-finite values.
Results may differ from a plain program's by a relative error of at most 0.0019.
Values may be sent and summed in bfloat16 or wider, within the bound.
A program may use at most 128 MiB of HBM per device.

v0:
```python
import jax
import jax.numpy as jnp
from jax import lax
from jax.sharding import PartitionSpec as P

CAP = 3


def slot_tiles(source, slot_block, slot_valid, owners):
    picked = jnp.take(source, slot_block.reshape(-1), axis=0)
    picked = picked.reshape(owners, CAP, source.shape[1], source.shape[2])
    return jnp.where(slot_valid[:, :, None, None] > 0, picked, jnp.zeros_like(picked))


def pair_block(received, first, second):
    return lax.dot_general(
        received[:, first],
        received[:, second],
        (((0, 2), (0, 2)), ((), ())),
        preferred_element_type=jnp.float32,
    )


def local(three_index, block_owner, pair_screen, orbital_counts, occupied_energy, virtual_energy):
    block_count, row_count, aux_local = three_index.shape
    occupied_width = occupied_energy.shape[1]
    virtual_width = virtual_energy.shape[1]
    groups = lax.axis_size("grp")
    owners = lax.axis_size("aux")
    own_index = lax.axis_index("aux")
    group_index = lax.axis_index("grp")
    quarter = row_count // groups
    owner_ids = jnp.arange(owners, dtype=jnp.int32)
    owned = (block_owner[None, :] == owner_ids[:, None]).astype(jnp.int32)
    slot_rank = jnp.cumsum(owned, axis=1) - 1
    slot_ids = jnp.arange(CAP, dtype=jnp.int32)
    selection = owned[:, None, :] * (slot_rank[:, None, :] == slot_ids[None, :, None]).astype(
        jnp.int32
    )
    block_ids = jnp.arange(block_count, dtype=jnp.int32)
    slot_block = jnp.sum(selection * block_ids[None, None, :], axis=2)
    slot_valid = jnp.sum(selection, axis=2)
    mine = lax.dynamic_index_in_dim(selection, own_index, 0, keepdims=False)
    my_block = jnp.sum(mine * block_ids[None, :], axis=1)
    my_valid = jnp.sum(mine, axis=1)
    energy = (virtual_energy[:, None, :] - occupied_energy[:, :, None]).reshape(
        block_count, row_count
    )
    occupied_flags = (
        jnp.arange(occupied_width, dtype=jnp.int32)[None, :] < orbital_counts[:, None]
    ).astype(jnp.float32)
    occupancy = jnp.repeat(occupied_flags, virtual_width, axis=1)
    slot_energy = jnp.take(energy, my_block, axis=0)
    slot_occupancy = jnp.take(occupancy, my_block, axis=0)
    screened = jnp.take(jnp.take(pair_screen, my_block, axis=0), my_block, axis=1)
    is_live = screened * my_valid[:, None] * my_valid[None, :] > 0

    def slot_amplitude(integral, first, second):
        energy_rows = lax.dynamic_slice_in_dim(slot_energy[first], group_index * quarter, quarter)
        occupied_rows = lax.dynamic_slice_in_dim(
            slot_occupancy[first], group_index * quarter, quarter
        )
        divisor = energy_rows[:, None] + slot_energy[second][None, :]
        return (
            occupied_rows[:, None] * slot_occupancy[second][None, :] * integral / divisor
        ).astype(jnp.bfloat16)

    def own_density(amplitude):
        row_form = amplitude.reshape(quarter // virtual_width, virtual_width, row_count)
        return jnp.einsum("iax,ibx->ab", row_form, row_form, preferred_element_type=jnp.float32)

    outgoing = slot_tiles(three_index, slot_block, slot_valid, owners)
    received = lax.all_to_all(outgoing, "aux", split_axis=0, concat_axis=0, tiled=True)
    zero_block = jnp.zeros((row_count, row_count), jnp.float32)
    empty = jnp.zeros((virtual_width, virtual_width), jnp.float32)
    pair_keys = [(first, second) for first in range(CAP) for second in range(first, CAP)]
    uppers = []
    for first, second in pair_keys:
        uppers.append(
            lax.cond(
                is_live[first, second],
                lambda first=first, second=second: pair_block(received, first, second),
                lambda: zero_block,
            )
        )
    slot_parts = [empty for first in range(CAP)]
    blocks = [[zero_block for second in range(CAP)] for first in range(CAP)]
    for index, (first, second) in enumerate(pair_keys):
        blocks[first][second] = uppers[index]
        blocks[second][first] = uppers[index].T
    stacked = jnp.stack([jnp.stack(line) for line in blocks])
    summed = lax.psum_scatter(stacked, "grp", scatter_dimension=2, tiled=True)
    for first in range(CAP):
        for second in range(CAP):

            def one_part(first=first, second=second):
                return own_density(slot_amplitude(summed[first, second], first, second))

            slot_parts[first] = slot_parts[first] + lax.cond(
                is_live[first, second], one_part, lambda: empty
            )
    spread = jnp.stack(slot_parts).reshape(CAP, groups, virtual_width // groups, virtual_width)
    placed = jnp.einsum(
        "cb,cgxy->gbxy", mine.astype(jnp.float32), spread, precision=lax.Precision.HIGHEST
    )
    placed = placed.reshape(groups * block_count, virtual_width // groups, virtual_width)
    return lax.psum_scatter(placed, ("grp", "aux"), scatter_dimension=0, tiled=True)


def solution(mesh):
    in_specs = (P(None, None, ("grp", "aux")), P(), P(), P(), P(), P())
    out_specs = P("aux", "grp", None)
    return jax.shard_map(local, mesh=mesh, in_specs=in_specs, out_specs=out_specs, check_vma=False)
```

profile of v0, /device:TPU:1, one launch (start us, length us, event | category | flops | bytes accessed | tf_op | source)
XLA Modules:
  0.0 1251.3 jit_solution(2966215952438917940)
XLA Ops:
  8.8 13.8 %gather_fusion.2 = bf16[96,768,128]{2,1,0:T(8,128)(2,1)} fusion(bf16[64,768,128]{2,1,0:T(8,128)(2,1)} %param.38, s32[1024]{0:T(1024)S(1)} %pad_clamp_fusion), kind=kCustom, calls=%fused_computation.4 | custom fusion | bytes 37749120 | tf_op jit(solution)/shard_map/jit(_take)/gather | solution.py:10
  22.5 17.3 %select_select_fusion = bf16[32,3,768,128]{3,2,1,0:T(8,128)(2,1)} fusion(bf16[32,3,768,128]{3,2,1,0:T(8,128)(2,1)} %bitcast.169, pred[32,3]{1,0:T(8,128)(4,1)S(1)} %get-tuple-element.242, pred[32,3]{1,0:T(8,128)(4,1)S(1)} %get-tuple-element.243), kind=kLoop, calls=%fused_computation.87 | loop fusion | flops 18874368 | bytes 37748928 | tf_op jit(solution)/shard_map/jit(_where)/select_n | solution.py:12
  39.9 8.6 all-to-all-start
  54.6 221.1 %all-to-all-done = bf16[32,3,768,128]{3,2,1,0:T(8,128)(2,1)} async-done(((bf16[32,3,768,128]{3,2,1,0:T(8,128)(2,1)}), bf16[32,3,768,128]{3,2,1,0:T(8,128)(2,1)}, u32[]{:S(2)}, u32[]{:S(2)}) %all-to-all-start) | async-done | bytes 18874400 | tf_op jit(solution)/shard_map/all_to_all | solution.py:73
  275.8 18.4 %copy.36 = bf16[32,3,768,128]{3,2,0,1:T(8,128)(2,1)} copy(bf16[32,3,768,128]{3,2,1,0:T(8,128)(2,1)} %all-to-all-done) | data formatting | bytes 37748736 | tf_op jit(solution)/shard_map/all_to_all | solution.py:73
  294.1 9.0 conditional.15
  294.1 9.0 fusion.3
  304.5 2.0 copy.37
  306.6 3.3 conditional.16
  306.6 1.6 broadcast_in_dim.59
  308.2 1.7 stack.49
  309.9 3.1 copy.40
  313.0 1.6 conditional.18
  313.0 1.6 broadcast_in_dim.64
  314.6 3.1 copy.42
  317.7 3.2 conditional.17
  317.7 1.6 broadcast_in_dim.62
  319.3 1.6 stack.51
  320.8 3.1 copy.44
  324.0 3.1 conditional.19
  325.5 1.6 stack.53
  327.1 3.1 copy.45
  330.2 1.5 conditional.20
  331.7 3.1 copy.47
  334.8 3.0 maximum_bitcast_fusion
  338.6 2.3 maximum_bitcast_fusion.1
  342.8 7.6 pad_maximum_fusion
  355.4 237.3 %reduce-scatter.3.cloned.1.call-done = f32[3,3,192,768]{3,2,1,0:T(8,128)} async-done(((f32[3,3,768,768]{3,2,1,0:T(8,128)}), f32[3,3,192,768]{3,2,1,0:T(8,128)}) %reduce-scatter.3.cloned.1.call-update) | async-done | bytes 5308432 | tf_op jit(solution)/shard_map/reduce_scatter | solution.py:92
  592.7 1.6 conditional.21
  594.9 2.0 convolution_bitcast_fusion.9
  597.0 2.0 copy.54
  599.0 644.2 %reduce-scatter.5.cloned.1.call-done = f32[2,12,48]{2,1,0:T(8,128)} async-done(((f32[256,12,48]{2,1,0:T(8,128)}), f32[2,12,48]{2,1,0:T(8,128)}) %reduce-scatter.5.cloned.1.call-update) | async-done | bytes 4624 | tf_op jit(solution)/shard_map/reduce_scatter | solution.py:107
  (85 shorter events, 18.3 us)
Async XLA Ops:
  6.5 42.3 %copy-start = (s32[64,64]{1,0:T(8,128)S(1)}, s32[64,64]{1,0:T(8,128)}, u32[]{:S(2)}) copy-start(s32[64,64]{1,0:T(8,128)} %param.40) | copy-start | bytes 49156
  39.9 235.9 %all-to-all-start = ((bf16[32,3,768,128]{3,2,1,0:T(8,128)(2,1)}), bf16[32,3,768,128]{3,2,1,0:T(8,128)(2,1)}, u32[]{:S(2)}, u32[]{:S(2)}) async-start(bf16[32,3,768,128]{3,2,1,0:T(8,128)(2,1)} %select_select_fusion), calls=%async_computation | async-start | bytes 37748736 | tf_op jit(solution)/shard_map/all_to_all | solution.py:73
  48.5 544.2 %reduce-scatter.3.cloned.1.call-start = ((), (), s32[]{:S(2)}) async-start(), calls=%async_computation.3 | async-start | bytes 26542080 | tf_op jit(solution)/shard_map/reduce_scatter | solution.py:92
  303.1 1.4 copy-start.7
  334.8 3.1 copy-start.2
  334.8 3.8 copy-start.3
  338.6 2.4 copy-start.4
  338.6 3.1 copy-start.5
  338.6 3.8 copy-start.6
  350.4 0.7 copy-start.8
  350.4 0.8 copy-start.9
  350.4 1.3 copy-start.10
  350.4 892.7 %reduce-scatter.5.cloned.1.call-start = ((), (), s32[]{:S(2)}) async-start(), calls=%async_computation.4 | async-start | bytes 2113536 | tf_op jit(solution)/shard_map/reduce_scatter | solution.py:107
  594.5 650.0 %copy-start.1 = (s32[64,64]{1,0:T(8,128)S(1)}, s32[64,64]{1,0:T(8,128)}, u32[]{:S(2)}) copy-start(s32[64,64]{1,0:T(8,128)} %param.40) | copy-start | bytes 49156
Sparse Core Ops, SparseCore 0:
  350.6 242.1 reduce-scatter.2
  599.1 644.0 reduce-scatter.4
where the time goes:
time: 1260 us; the launch traced here: 1250 us
  waiting for transfers between devices  1100 us (87%)
  local copies, waits for them, and re-layouts  74.2 us (6%)
  other arithmetic  34.7 us (3%)
  between operations  19.3 us (2%)
    reduce_scatter x1, waiting for transfers between devices, local(): lax.psum_scatter(placed, ('grp', 'aux'), scatter_dimension=0, tiled=True)  644 us
    reduce_scatter x1, waiting for transfers between devices, local(): summed = lax.psum_scatter(stacked, 'grp', scatter_dimension=2, tiled=True)  237 us
    all_to_all x1, waiting for transfers between devices, local(): lax.all_to_all(outgoing, 'aux', split_axis=0, concat_axis=0, tiled=True)  221 us
  transfers between devices with their start and end apart: 3, of which 3 were waited for; matrix products, arithmetic and copies ran while one was open for 0% of the time, Pallas kernels for 0%

commit v1 on v0

v1 whole, which is shorter than its diff:
```python
import functools

import jax
import jax.numpy as jnp
import numpy as np
from jax import lax
from jax.experimental import pallas as pl
from jax.experimental.pallas import tpu as pltpu
from jax.sharding import PartitionSpec as P

NV = 48
OB = 16
BINS = 16
GROUP = 8
ROWS = GROUP * NV
SIDE = 4
PART_A = 6
ALL = (0, BINS)
ROOMY = (((ALL,) * 6), ((ALL,) * 4))
TIGHT = ((ALL, ALL, ALL, (0, 15), (0, 9), (0, 4)), (ALL, (2, BINS)))
MESH = pl.DeviceIdType.MESH
VMEM = pl.BlockSpec(memory_space=pltpu.VMEM)
SMEM = pl.BlockSpec(memory_space=pltpu.SMEM)
ANY = pl.BlockSpec(memory_space=pl.ANY)


def has(limits, index):
    first, end = limits
    return (index >= first) & (index < end)


def plan(block_owner, orbital_counts):
    ids = jnp.arange(block_owner.shape[0], dtype=jnp.int32)
    same = block_owner[:, None] == block_owner[None, :]
    earlier = same & (ids[None, :] < ids[:, None])
    load = jnp.sum(jnp.where(same, orbital_counts[None, :], 0), axis=1)
    base = jnp.sum(jnp.where(earlier, orbital_counts[None, :], 0), axis=1)
    first = jnp.sum(earlier.astype(jnp.int32), axis=1) == 0
    ahead = (load[None, :] > load[:, None]) | (
        (load[None, :] == load[:, None]) & (block_owner[None, :] < block_owner[:, None])
    )
    rank = jnp.sum((ahead & first[None, :]).astype(jnp.int32), axis=1)
    second = rank >= BINS
    bin_of = jnp.where(second, 2 * BINS - 1 - rank, rank)
    local = base + jnp.where(second, PART_A * GROUP, 0)
    room = jnp.zeros_like(load)
    for part, limits in enumerate(TIGHT):
        for limit in limits:
            room = room + jnp.where(second == (part == 1), has(limit, bin_of) * GROUP, 0)
    return bin_of, local, jnp.all(load <= room)


def pack_kernel(slots, start_ref, count_ref, source, packed, sem):
    def copies(block, act):
        count = count_ref[block]
        start = start_ref[block]
        for size in (16, 8, 4, 2, 1):
            offset = (count // (2 * size)) * (2 * size)

            @pl.when((count // size) % 2 == 1)
            def _(size=size, offset=offset):
                act(
                    pltpu.make_async_copy(
                        source.at[pl.ds(block * OB + offset, size)],
                        packed.at[pl.ds(start + offset, size)],
                        sem,
                    )
                )

    @pl.loop(0, source.shape[0] // OB)
    def _(block):
        copies(block, lambda copy: copy.start())

    @pl.loop(0, source.shape[0] // OB)
    def _(block):
        copies(block, lambda copy: copy.wait())


def position():
    z = lax.axis_index("grp")
    aux = lax.axis_index("aux")
    core = lax.rem(aux, 2)
    x = lax.rem(aux // 2, SIDE)
    y = aux // (2 * SIDE)
    return x, y, z, core


def device(x, y, z, core):
    return (z, (y * SIDE + x) * 2 + core)


def bin_index(x, y, z, core):
    kind = lax.rem(x, 2) + 2 * lax.rem(y, 2) + 4 * lax.rem(z, 2)
    return kind + core * (BINS - 1 - 2 * kind)


def shifted(value, by):
    return lax.rem(value + by + SIDE, SIDE)


def gram_kernel(
    limits,
    packed,
    out,
    held,
    tiles,
    parts,
    send_sem,
    recv_sem,
    local_sem,
    tile_send,
    tile_recv,
    out_buf,
    out_sem,
    exact,
    exact_parts,
    exact_send,
    exact_recv,
):
    x, y, z, core = position()
    sign = 1 - 2 * core
    own_bin = bin_index(x, y, z, core)
    own_part = x // 2 + 2 * (y // 2) + 4 * (z // 2)
    counts = [len(limits[0]), len(limits[1])]
    limits = limits[0] + limits[1]
    groups = len(limits)
    bits = [(d % 2, (d // 2) % 2, d // 4) for d in range(8)]

    barrier = pltpu.get_barrier_semaphore()

    def greet(target):
        pl.semaphore_signal(barrier, inc=1, device_id=target, device_id_type=MESH)

    greet(device(x, y, z, 1 - core))
    for d in range(1, 8):
        dx, dy, dz = bits[d]
        greet(device(shifted(x, -dx), shifted(y, -dy), shifted(z, -dz), 0))
        greet(device(shifted(x, dx), shifted(y, dy), shifted(z, dz), 1))
        greet(device(shifted(x, 2 * dx), shifted(y, 2 * dy), shifted(z, 2 * dz), core))
    pl.semaphore_wait(barrier, 22)

    def gather(d, target_core, group, act):
        dx, dy, dz = bits[d]
        tx, ty, tz = shifted(x, sign * dx), shifted(y, sign * dy), shifted(z, sign * dz)
        target_bin = bin_index(tx, ty, tz, target_core)
        copy = pltpu.make_async_remote_copy(
            src_ref=packed.at[target_bin, group],
            dst_ref=held.at[2 * d + core, group],
            send_sem=send_sem.at[2 * d + target_core, group],
            recv_sem=recv_sem.at[2 * d + core, group],
            device_id=device(tx, ty, tz, target_core),
            device_id_type=MESH,
        )
        when(group, target_bin, lambda: act(copy))

    def when(group, index, act):
        if limits[group] == ALL:
            act()
        else:
            pl.when(has(limits[group], index))(act)

    def keep(group):
        return pltpu.make_async_copy(
            packed.at[own_bin, group], held.at[core, group], local_sem.at[group]
        )

    for group in range(groups):
        when(group, own_bin, lambda: keep(group).start())
        for d in range(1, 8):
            for target_core in range(2):
                gather(d, target_core, group, lambda copy: copy.start())
        gather(0, 1 - core, group, lambda copy: copy.start())

    def arrived(group):
        keep(group).wait()
        pltpu.make_async_copy(
            held.at[1 - core, group], held.at[1 - core, group], recv_sem.at[1 - core, group]
        ).wait()
        for source in range(2, BINS):
            pltpu.make_async_copy(
                held.at[source, group], held.at[source, group], recv_sem.at[source, group]
            ).wait()

    def rows_of(group):
        return jnp.concatenate([held[source, group] for source in range(BINS)], axis=1)

    def scatter(e, first, count, column):
        dx, dy, dz = bits[e]
        px, py, pz = shifted(x, 2 * dx), shifted(y, 2 * dy), shifted(z, 2 * dz)
        part = px // 2 + 2 * (py // 2) + 4 * (pz // 2)
        return pltpu.make_async_remote_copy(
            src_ref=tiles.at[part, pl.ds(first, count)],
            dst_ref=parts.at[e - 1, pl.ds(first, count)],
            send_sem=tile_send.at[e - 1, column],
            recv_sem=tile_recv.at[e - 1, column],
            device_id=device(px, py, pz, core),
            device_id_type=MESH,
        )

    columns = []
    first = 0
    for base, count in ((0, counts[0]), (counts[0], counts[1])):
        for v in range(count):
            columns.append((base, v, first))
            first += v + 1
    same_row = lax.broadcasted_iota(jnp.int32, (ROWS, ROWS), 0) == lax.broadcasted_iota(
        jnp.int32, (ROWS, ROWS), 1
    )

    def make_column(column, base, v, first):
        arrived(base + v)

        @pl.loop(0, v + 1)
        def _(u):
            tile = lax.dot_general(
                rows_of(base + u),
                rows_of(base + v),
                (((1,), (1,)), ((), ())),
                preferred_element_type=jnp.float32,
            )

            @pl.when(u == v)
            def _():
                exact[pl.ds(column, 1), :] = jnp.sum(
                    jnp.where(same_row, tile, 0.0), axis=0, keepdims=True
                )

            rounded = tile.astype(jnp.bfloat16)
            for part in range(8):
                tiles[part, first + u] = rounded[part * NV : (part + 1) * NV]

        for e in range(1, 8):
            scatter(e, first, v + 1, column).start()

    for column, (base, v, first) in enumerate(columns):
        when(column, own_bin, functools.partial(make_column, column, base, v, first))

    def scatter_exact(e):
        dx, dy, dz = bits[e]
        px, py, pz = shifted(x, 2 * dx), shifted(y, 2 * dy), shifted(z, 2 * dz)
        return pltpu.make_async_remote_copy(
            src_ref=exact,
            dst_ref=exact_parts.at[e - 1],
            send_sem=exact_send.at[e - 1],
            recv_sem=exact_recv.at[e - 1],
            device_id=device(px, py, pz, core),
            device_id_type=MESH,
        )

    for e in range(1, 8):
        scatter_exact(e).start()
    for e in range(1, 8):
        scatter_exact(e).wait()
    exact[...] = exact[...] + jnp.sum(exact_parts[...], axis=0)
    own_diagonal = (
        lax.broadcasted_iota(jnp.int32, (NV, ROWS), 0) + own_part * NV
        == lax.broadcasted_iota(jnp.int32, (NV, ROWS), 1)
    )

    def add_column(column, base, v, first):
        for e in range(1, 8):
            scatter(e, first, v + 1, column).wait_recv()

        @pl.loop(first, first + v + 1)
        def _(index):
            total = tiles[own_part, index].astype(jnp.float32)
            for e in range(7):
                total = total + parts[e, index].astype(jnp.float32)
            out_buf[index] = total

        out_buf[first + v] = jnp.where(own_diagonal, exact[pl.ds(column, 1), :], out_buf[first + v])

    for column, (base, v, first) in enumerate(columns):
        when(column, own_bin, functools.partial(add_column, column, base, v, first))

    done = pltpu.make_async_copy(out_buf, out, out_sem)
    done.start()

    def sent_column(column, base, v, first):
        for e in range(1, 8):
            scatter(e, first, v + 1, column).wait_send()

    for column, (base, v, first) in enumerate(columns):
        when(column, own_bin, functools.partial(sent_column, column, base, v, first))
    for group in range(groups):
        gather(0, 1 - core, group, lambda copy: copy.wait_send())
        for d in range(1, 8):
            for target_core in range(2):
                gather(d, target_core, group, lambda copy: copy.wait_send())
    done.wait()


def density_kernel(counts, block_ref, part_ref, strips, row_energy, column_energy, mask, density, fold):
    part = part_ref[0]
    density[...] = jnp.zeros_like(density)
    row_slot = lax.broadcasted_iota(jnp.int32, (ROWS, ROWS), 0) // NV
    column_slot = lax.broadcasted_iota(jnp.int32, (ROWS, ROWS), 1) // NV
    diagonal = row_slot == column_slot
    fold[...] = (
        lax.rem(lax.broadcasted_iota(jnp.int32, (ROWS, NV), 0), NV)
        == lax.broadcasted_iota(jnp.int32, (ROWS, NV), 1)
    ).astype(jnp.float32)
    first = 0
    for base, count in ((0, counts[0]), (counts[0], counts[1])):
        row_sums = [jnp.zeros((NV, NV), jnp.float32) for u in range(count)]
        for v in range(count):
            stack = []
            for u in range(v + 1):
                kind = mask[base + u, base + v]
                quotient = strips[first + u] / (row_energy[base + u] + column_energy[base + v])
                amplitude = jnp.where(kind > 0, quotient, 0.0).astype(jnp.bfloat16)
                row_sums[u] = row_sums[u] + lax.dot_general(
                    amplitude, amplitude, (((1,), (1,)), ((), ())), preferred_element_type=jnp.float32
                )
                if u == v:
                    amplitude = jnp.where(kind > 1, quotient, 0.0).astype(jnp.bfloat16)
                stack.append(amplitude)
            first += v + 1
            stacked = jnp.concatenate(stack, axis=0)
            product = lax.dot_general(
                stacked, stacked, (((0,), (0,)), ((), ())), preferred_element_type=jnp.float32
            )
            folded = jnp.dot(
                jnp.where(diagonal, product, 0.0),
                fold[...],
                precision=lax.Precision.HIGHEST,
                preferred_element_type=jnp.float32,
            )
            for j in range(GROUP):
                block = block_ref[(base + v) * GROUP + j]
                density[block] = density[block] + folded[j * NV : (j + 1) * NV]
        for u in range(count):
            block = block_ref[(base + u) * GROUP + part]
            density[block] = density[block] + row_sums[u]


def exchange_kernel(spread, out, held, total, summed, z_send, z_recv, send_sem, recv_sem):
    z = lax.axis_index("grp")
    aux = lax.axis_index("aux")
    groups = lax.axis_size("grp")
    owners = lax.axis_size("aux")
    rows = out.shape[0]
    barrier = pltpu.get_barrier_semaphore()
    for step in range(1, groups):
        pl.semaphore_signal(
            barrier, inc=1, device_id=(lax.rem(z + step, groups), aux), device_id_type=MESH
        )

    @pl.loop(1, owners)
    def _(step):
        pl.semaphore_signal(
            barrier, inc=1, device_id=(z, lax.rem(aux + step, owners)), device_id_type=MESH
        )

    pl.semaphore_wait(barrier, groups + owners - 2)

    def across(step):
        target = lax.rem(z + step, groups)
        return pltpu.make_async_remote_copy(
            src_ref=spread.at[target],
            dst_ref=held.at[step - 1],
            send_sem=z_send.at[step - 1],
            recv_sem=z_recv.at[step - 1],
            device_id=(target, aux),
            device_id_type=MESH,
        )

    for step in range(1, groups):
        across(step).start()
    for step in range(1, groups):
        across(step).wait_recv()
    total[...] = spread[z] + held[0] + held[1] + held[2]

    def along(step):
        target = lax.rem(aux + step, owners)
        return pltpu.make_async_remote_copy(
            src_ref=total.at[pl.ds(pl.multiple_of(target * rows, rows), rows)],
            dst_ref=summed.at[step],
            send_sem=send_sem.at[step],
            recv_sem=recv_sem.at[step],
            device_id=(z, target),
            device_id_type=MESH,
        )

    @pl.loop(1, owners)
    def _(step):
        along(step).start()

    summed[0] = total[pl.ds(pl.multiple_of(aux * rows, rows), rows), :]

    @pl.loop(1, owners)
    def _(step):
        along(step).wait_recv()

    out[...] = jnp.sum(summed[...], axis=0)

    @pl.loop(1, owners)
    def _(step):
        along(step).wait_send()

    for step in range(1, groups):
        across(step).wait_send()


def partial_density(
    limits,
    collective_id,
    bin_of,
    start,
    three_index,
    pair_screen,
    orbital_counts,
    occupied_energy,
    virtual_energy,
):
    blocks, row_count, aux_local = three_index.shape
    counts = [len(part) for part in limits]
    groups = sum(counts)
    slots = groups * GROUP
    tile_count = sum(count * (count + 1) // 2 for count in counts)

    packed = pl.pallas_call(
        functools.partial(pack_kernel, slots),
        out_shape=jax.ShapeDtypeStruct((BINS * slots, NV, aux_local), jnp.bfloat16),
        in_specs=[SMEM, SMEM, ANY],
        out_specs=ANY,
        scratch_shapes=[pltpu.SemaphoreType.DMA],
    )(bin_of * slots + start, orbital_counts, three_index.reshape(blocks * OB, NV, aux_local))

    strips = pl.pallas_call(
        functools.partial(gram_kernel, limits),
        out_shape=jax.ShapeDtypeStruct((tile_count, NV, ROWS), jnp.float32),
        in_specs=[ANY],
        out_specs=ANY,
        scratch_shapes=[
            pltpu.VMEM((BINS, groups, ROWS, aux_local), jnp.bfloat16),
            pltpu.VMEM((8, tile_count, NV, ROWS), jnp.bfloat16),
            pltpu.VMEM((7, tile_count, NV, ROWS), jnp.bfloat16),
            pltpu.SemaphoreType.DMA((BINS, groups)),
            pltpu.SemaphoreType.DMA((BINS, groups)),
            pltpu.SemaphoreType.DMA((groups,)),
            pltpu.SemaphoreType.DMA((7, groups)),
            pltpu.SemaphoreType.DMA((7, groups)),
            pltpu.VMEM((tile_count, NV, ROWS), jnp.float32),
            pltpu.SemaphoreType.DMA,
            pltpu.VMEM((16, ROWS), jnp.float32),
            pltpu.VMEM((7, 16, ROWS), jnp.float32),
            pltpu.SemaphoreType.DMA((7,)),
            pltpu.SemaphoreType.DMA((7,)),
        ],
        compiler_params=pltpu.CompilerParams(
            collective_id=collective_id, has_side_effects=True, vmem_limit_bytes=58 * 2**20
        ),
    )(packed.reshape(BINS, groups, ROWS, aux_local))

    x, y, z, core = position()
    own_bin = bin_index(x, y, z, core)
    own_part = x // 2 + 2 * (y // 2) + 4 * (z // 2)
    slot_ids = jnp.arange(slots, dtype=jnp.int32)
    inside = (
        (bin_of[None, :] == own_bin)
        & (start[None, :] <= slot_ids[:, None])
        & (slot_ids[:, None] < (start + orbital_counts)[None, :])
    )
    pick = inside.astype(jnp.float32)
    slot_block = jnp.sum(jnp.where(inside, jnp.arange(blocks, dtype=jnp.int32)[None, :], 0), axis=1)
    orbital = slot_ids[:, None] - start[None, :]
    occupied = jnp.sum(
        jnp.where(
            inside[:, :, None] & (orbital[:, :, None] == jnp.arange(OB, dtype=jnp.int32)),
            occupied_energy[None],
            0.0,
        ),
        axis=(1, 2),
    )
    energy = (
        jnp.sum(jnp.where(inside[:, :, None], virtual_energy[None], 0.0), axis=1) - occupied[:, None]
    )
    row_pick = lax.dynamic_index_in_dim(pick.reshape(groups, GROUP, blocks), own_part, 1, False)
    row_energy = lax.dynamic_index_in_dim(energy.reshape(groups, GROUP, NV), own_part, 1, False)
    screen = (pair_screen == 1).astype(jnp.float32)
    live = jnp.dot(jnp.dot(row_pick, screen), pick.T)
    row_ids = jnp.arange(groups, dtype=jnp.int32) * GROUP + own_part
    kind = jnp.where(
        live > 0.5,
        jnp.where(row_ids[:, None] < slot_ids, 2.0, jnp.where(row_ids[:, None] == slot_ids, 1.0, 0.0)),
        0.0,
    )
    kind = jnp.broadcast_to(kind.reshape(groups, groups, 1, GROUP, 1), (groups, groups, 1, GROUP, NV))

    return pl.pallas_call(
        functools.partial(density_kernel, counts),
        out_shape=jax.ShapeDtypeStruct((blocks, NV, NV), jnp.float32),
        in_specs=[SMEM, SMEM, VMEM, VMEM, VMEM, VMEM],
        out_specs=VMEM,
        scratch_shapes=[pltpu.VMEM((ROWS, NV), jnp.float32)],
        compiler_params=pltpu.CompilerParams(vmem_limit_bytes=40 * 2**20),
    )(
        slot_block,
        own_part.reshape(1),
        strips,
        row_energy.reshape(groups, NV, 1),
        energy.reshape(groups, 1, ROWS),
        kind.reshape(groups, groups, 1, ROWS),
    )


def local(three_index, block_owner, pair_screen, orbital_counts, occupied_energy, virtual_energy):
    bin_of, start, fits = plan(block_owner, orbital_counts)
    density = lax.cond(
        fits,
        functools.partial(partial_density, TIGHT, 0),
        functools.partial(partial_density, ROOMY, 2),
        bin_of,
        start,
        three_index,
        pair_screen,
        orbital_counts,
        occupied_energy,
        virtual_energy,
    )

    groups_z = lax.axis_size("grp")
    owners = lax.axis_size("aux")
    width = NV // groups_z
    spread = density.reshape(owners, 2, groups_z, width, NV).transpose(2, 0, 3, 1, 4)
    spread = jnp.pad(spread, ((0, 0), (0, 0), (0, 16 - width), (0, 0), (0, 64 - NV)))
    spread = spread.reshape(groups_z, owners * 16, 128)
    home = pl.pallas_call(
        exchange_kernel,
        out_shape=jax.ShapeDtypeStruct((16, 128), jnp.float32),
        in_specs=[VMEM],
        out_specs=VMEM,
        scratch_shapes=[
            pltpu.VMEM((groups_z - 1, owners * 16, 128), jnp.float32),
            pltpu.VMEM((owners * 16, 128), jnp.float32),
            pltpu.VMEM((owners, 16, 128), jnp.float32),
            pltpu.SemaphoreType.DMA((groups_z - 1,)),
            pltpu.SemaphoreType.DMA((groups_z - 1,)),
            pltpu.SemaphoreType.DMA((owners,)),
            pltpu.SemaphoreType.DMA((owners,)),
        ],
        compiler_params=pltpu.CompilerParams(
            collective_id=1, has_side_effects=True, vmem_limit_bytes=32 * 2**20
        ),
    )(spread)
    return home.reshape(16, 2, 64)[:width, :, :NV].transpose(1, 0, 2)


def solution(mesh):
    in_specs = (P(None, None, ("grp", "aux")), P(), P(), P(), P(), P())
    out_specs = P("aux", "grp", None)
    return jax.shard_map(local, mesh=mesh, in_specs=in_specs, out_specs=out_specs, check_vma=False)
```

time: 1260 us -> 433 us (0.34)
  waiting for transfers between devices: 1100 us -> 0 us
  Pallas kernels: 0 us -> 407 us
  local copies, waits for them, and re-layouts: 74.2 us -> 8.01 us
  other arithmetic: 34.7 us -> 5 us
  between operations: 19.3 us -> 0.94 us
    reduce_scatter x2 -> x0, waiting for transfers between devices: 882 us -> none  [the longest x1 644 us: local(): lax.psum_scatter(placed, ('grp', 'aux'), scatter_dimension=0, tiled=True)]
    pallas_call x0 -> x4, Pallas kernels: none -> 407 us  [the longest x1 223 us: partial_density(): pl.pallas_call(functools.partial(pack_kernel, slots), out_shape=jax.Shape...]
    all_to_all x1 -> x0, waiting for transfers between devices: 221 us -> none  [local(): lax.all_to_all(outgoing, 'aux', split_axis=0, concat_axis=0, tiled=True)]
    all_to_all x1 -> x0, local copies, waits for them, and re-layouts: 18.4 us -> none  [local(): lax.all_to_all(outgoing, 'aux', split_axis=0, concat_axis=0, tiled=True)]
    select_n x6 -> x0, other arithmetic: 17.5 us -> none  [the longest x1 17.3 us: slot_tiles(): jnp.where(slot_valid[:, :, None, None] > 0, picked, jnp.zeros_like(picked))]
    gather x5 -> x0, local copies, waits for them, and re-layouts: 16 us -> none  [the longest x1 13.8 us: slot_tiles(): picked = jnp.take(source, slot_block.reshape(-1), axis=0)]
    cond x6 -> x9, local copies, waits for them, and re-layouts: 17.5 us -> 3.4 us  [the longest x1 1.92 us: local(): lax.cond(fits, functools.partial(partial_density, TIGHT, 0), functools.pa...]
    another operation x5 -> x0, other arithmetic: 13.5 us -> none  [the longest x4 13.3 us: local(): stacked = jnp.stack([jnp.stack(line) for line in blocks])]
  transfers between devices with their start and end apart: 3 -> 0, of which waited for: 3 -> 0; matrix products, arithmetic and copies ran while one was open for 0% -> 0% of each run, Pallas kernels for 0% -> 0%
where the time goes in v1:
time: 433 us; the launch traced here: 427 us
  Pallas kernels  407 us (94%)
  local copies, waits for them, and re-layouts  8.01 us (2%)
  loops' own time  5.8 us (1%)
  other arithmetic  5 us (1%)
    pallas_call x1, Pallas kernels, partial_density(): pl.pallas_call(functools.partial(pack_kernel, slots), out_shape=jax.Shape...  223 us
    pallas_call x1, Pallas kernels, partial_density(): pl.pallas_call(functools.partial(gram_kernel, limits), out_shape=jax.Shap...  115 us
    pallas_call x1, Pallas kernels, local(): pl.pallas_call(exchange_kernel, out_shape=jax.ShapeDtypeStruct((16, 128),...  61.3 us

profile of v1, /device:TPU:1, one launch (start us, length us, event | category | flops | bytes accessed | tf_op | source)
XLA Modules:
  0.0 427.0 jit_solution(6461953539505693319)
XLA Ops:
  0.0 0.9 select_reduce_fusion.6
  1.0 0.9 convert_reduce_fusion
  1.9 0.7 compare_reduce_fusion
  3.2 356.7 %conditional.1 = (f32[64,48,48]{2,1,0:T(8,128)}) conditional(s32[]{:T(128)} %convert_element_type.9, (s32[64]{0:T(128)S(1)}, s32[64]{0:T(128)S(1)}, s32[64]{0:T(128)}, bf16[64,768,128]{2,1,0:T(8,128)(2,1)}, f32[64,48]{0,1:T(8,128)}, /*index=5*/f32[64,16]{0,1:T(8,128)}, s32[64,64]{1,0:T(8,128)}) %tuple.11, (s32[64]{0:T(128)S(1)}, s32[64]{0:T(128)S(1)}, ...), branch_computations={%region_5.9_spmd, %region_9.13_spmd} | conditional | flops 1092628 | bytes 10058544 | solution.py:510
  8.6 1.2 multiply_add_fusion.5
  9.8 0.1 iota_subtract_fusion.1
  10.0 223.3 %branch_1_fun.3 = bf16[1024,48,128]{2,1,0:T(8,128)(2,1)} custom-call(s32[64]{0:T(128)} %get-tuple-element.115.start_ref, s32[64]{0:T(128)} %get-tuple-element.45.count_ref, bf16[1024,48,128]{2,1,0:T(8,128)(2,1)} %bitcast.31), custom_call_target="tpu_custom_call" | custom-call | tf_op jit(solution)/shard_map/cond/branch_1_fun/pallas_call | solution.py:422
  233.3 0.0 copy-start.5
  233.3 0.0 copy-start.7
  233.3 114.5 %branch_1_fun.4.strips = f32[24,48,384]{2,1,0:T(8,128)} custom-call(bf16[16,8,384,128]{3,2,1,0:T(8,128)(2,1)} %bitcast.32), custom_call_target="tpu_custom_call" | custom-call | tf_op jit(solution)/shard_map/cond/branch_1_fun/pallas_call | solution.py:430
  347.9 0.5 select_reduce_fusion.3
  348.4 0.6 select_reduce_fusion.4
  348.9 0.1 sub.106
  349.0 0.1 constant_dynamic-slice_fusion.3
  349.1 0.1 dynamic-slice_subtract_fusion.1
  349.2 0.1 copy.57.row_energy
  349.3 0.1 reduce_sum.103
  349.4 0.1 sub.107
  349.5 0.1 sub.109
  349.7 0.3 fusion.44
  350.0 0.1 broadcast_in_dim.206
  350.0 0.1 broadcast_in_dim.207
  350.2 0.3 broadcast_in_dim.208.mask
  350.4 1.5 copy-done.1
  351.9 7.8 %branch_1_fun.5 = f32[64,48,48]{2,1,0:T(8,128)} custom-call(s32[64]{0:T(128)S(1)} %get-tuple-element.114.block_ref, s32[1]{0:T(128)} %bitcast.7.part_ref, f32[24,48,384]{2,1,0:T(8,128)S(1)} %copy-done.1, f32[8,48,1]{2,1,0:T(8,128)S(1)} %copy.57.row_energy, f32[8,1,384]{2,1,0:T(1,128)S(1)} %sub.110.column_energy, f32[8,8,1,384]{3,2,1,0:T(1,128)S(1)} %broadcast_in_dim.208.mask), custom_call_target="tpu_custom_call" | custom-call | tf_op jit(solution)/shard_map/cond/branch_1_fun/pallas_call | solution.py:491
  359.9 1.9 copy.60
  361.9 0.5 copy.62
  362.4 1.2 pad.4.clone
  363.6 1.1 reshape.314.spread
  364.8 61.3 %shard_map.64 = f32[16,128]{1,0:T(8,128)S(1)} custom-call(f32[4,512,128]{2,1,0:T(8,128)S(1)} %reshape.314.spread), custom_call_target="tpu_custom_call" | custom-call | tf_op jit(solution)/shard_map/pallas_call | solution.py:529
  426.1 0.1 reshape.315
  426.2 0.6 slice_bitcast_fusion
  (13 shorter events, 0.1 us)
Async XLA Ops:
  233.3 114.6 %copy-start.3 = (f32[64,48]{0,1:T(8,128)S(1)}, f32[64,48]{0,1:T(8,128)}, u32[]{:S(2)}) copy-start(f32[64,48]{0,1:T(8,128)} %get-tuple-element.47) | copy-start | bytes 36868 | tf_op jit(solution)/shard_map/cond
  233.3 115.1 %copy-start.5 = (f32[64,16]{0,1:T(8,128)S(1)}, f32[64,16]{0,1:T(8,128)}, u32[]{:S(2)}) copy-start(f32[64,16]{0,1:T(8,128)} %get-tuple-element.48) | copy-start | bytes 12292 | tf_op jit(solution)/shard_map/cond
  233.3 116.4 %copy-start.7 = (s32[64,64]{1,0:T(8,128)S(1)}, s32[64,64]{1,0:T(8,128)}, u32[]{:S(2)}) copy-start(s32[64,64]{1,0:T(8,128)} %get-tuple-element.49) | copy-start | bytes 49156 | tf_op jit(solution)/shard_map/cond
  350.4 1.5 copy-start.1
